TPU v7x, 256 devices: a whole 4x4x8 slice. The times are simulated.
256 devices in a mesh: dp: 32 (over x, z), tensor: 8 (over y, core).
Axes of the slice: x: 4, y: 4, z: 8, core: 2. Of those that a mesh axis runs over, the one named last changes fastest.
Arguments:
- tokens: bfloat16 [1024, 6144], P('dp', 'tensor'), may hold values from -32 to 32
- gain_in: float32 [6144], P('tensor'), may hold values from 0.1 to 1.9
- shift_in: float32 [6144], P('tensor'), may hold values from -3 to 3
- up_weight: bfloat16 [6144, 24576], P('tensor', 'dp'), may hold values from -0.078125 to 0.078125
- up_bias: float32 [24576], P('dp'), may hold values from -3 to 3
- down_weight: bfloat16 [24576, 6144], P('dp', 'tensor'), may hold values from -1 to 1
- gain_out: float32 [6144], P('tensor'), may hold values from 0.1 to 1.9
- curvature: float32 [1024, 6144], P('dp', 'tensor'), may hold values from 0.5 to 12
- up_tangent: bfloat16 [6144, 24576], P('tensor', 'dp'), may hold values from -0.078125 to 0.078125
- down_tangent: bfloat16 [24576, 6144], P('dp', 'tensor'), may hold values from -1 to 1
Outputs:
- up_product: float32 [6144, 24576], P('tensor', 'dp')
- down_product: float32 [24576, 6144], P('dp', 'tensor')
All inputs are finite; a program needn't handle non-finite values.
Results may differ from a plain program's by a relative error of at most 0.003.
Values may be sent and summed in bfloat16 or wider, within the bound.
A program may use at most 128 MiB of HBM per device.

v0:
```python
import jax
import jax.numpy as jnp
from jax import lax
from jax.sharding import PartitionSpec as P

D = 6144
epsilon = 1e-05
root_half = 0.7071067811865476
inv_root_two_pi = 0.3989422804014327


def gelu_value(values):
    return 0.5 * values * (1.0 + lax.erf(values * root_half))


def gelu_slope(values):
    return (
        0.5 * (1.0 + lax.erf(values * root_half))
        + values * jnp.exp(-0.5 * values * values) * inv_root_two_pi
    )


def row_total(values):
    return jnp.sum(values, axis=1)


def on_device(
    tokens,
    gain_in,
    shift_in,
    up_weight,
    up_bias,
    down_weight,
    gain_out,
    curvature,
    up_tangent,
    down_tangent,
):
    model_width = float(D)
    source = tokens.astype(jnp.float32)
    sum_in, square_in = lax.psum((row_total(source), row_total(source * source)), "tensor")
    center_in = sum_in / model_width
    spread_in = square_in / model_width - center_in * center_in
    inverse_in = lax.rsqrt(spread_in + epsilon)[:, None]
    normed = ((source - center_in[:, None]) * inverse_in * gain_in + shift_in).astype(jnp.bfloat16)
    all_normed = lax.all_gather(normed, "dp", axis=0, tiled=True)
    pre_part = jnp.dot(all_normed, up_weight, preferred_element_type=jnp.float32)
    tangent_part = jnp.dot(all_normed, up_tangent, preferred_element_type=jnp.float32)
    share_rows = all_normed.shape[0] // lax.axis_size("tensor")
    pre_total, tangent_total = lax.psum((pre_part, tangent_part), "tensor")
    pre_full = pre_total + up_bias
    slope_full = gelu_slope(pre_full)
    hidden = gelu_value(pre_full).astype(jnp.bfloat16)
    hidden_tangent = (slope_full * tangent_total).astype(jnp.bfloat16)
    slope_rows = lax.dynamic_slice_in_dim(
        slope_full, lax.axis_index("tensor") * share_rows, share_rows, 0
    )
    slope_kept = lax.optimization_barrier(slope_rows.astype(jnp.bfloat16))
    primal = jnp.dot(hidden, down_weight, preferred_element_type=jnp.float32)
    tangent = jnp.dot(hidden_tangent, down_weight, preferred_element_type=jnp.float32) + jnp.dot(
        hidden, down_tangent, preferred_element_type=jnp.float32
    )
    both_outputs = lax.psum_scatter(
        jnp.concatenate([primal, tangent], axis=1), "dp", scatter_dimension=0, tiled=True
    )
    local_width = down_weight.shape[1]
    output = source + both_outputs[:, :local_width]
    output_tangent = both_outputs[:, local_width:]
    factor = gain_out * gain_out * curvature
    sum_out, square_out = lax.psum((row_total(output), row_total(output * output)), "tensor")
    center_out = sum_out / model_width
    inverse_out = lax.rsqrt(square_out / model_width - center_out * center_out + epsilon)[:, None]
    normal_out = (output - center_out[:, None]) * inverse_out
    tangent_sum, tangent_dot = lax.psum(
        (row_total(output_tangent), row_total(normal_out * output_tangent)), "tensor"
    )
    normal_tangent = (
        output_tangent
        - (tangent_sum / model_width)[:, None]
        - normal_out * (tangent_dot / model_width)[:, None]
    ) * inverse_out
    weighted = factor * normal_tangent
    weight_sum, weight_dot = lax.psum(
        (row_total(weighted), row_total(normal_out * weighted)), "tensor"
    )
    cotangent = (
        (
            weighted
            - (weight_sum / model_width)[:, None]
            - normal_out * (weight_dot / model_width)[:, None]
        )
        * inverse_out
    ).astype(jnp.bfloat16)
    all_cotangent = lax.all_gather(cotangent, "dp", axis=0, tiled=True)
    back_part = lax.dot_general(
        all_cotangent, down_weight, (((1,), (1,)), ((), ())), preferred_element_type=jnp.float32
    )
    down_product = lax.dot_general(
        hidden, all_cotangent, (((0,), (0,)), ((), ())), preferred_element_type=jnp.float32
    )
    back_share = lax.psum_scatter(back_part, "tensor", scatter_dimension=0, tiled=True)
    grad_share = (back_share * slope_kept.astype(jnp.float32)).astype(jnp.bfloat16)
    grad_pre = lax.all_gather(grad_share, "tensor", axis=0, tiled=True)
    up_product = lax.dot_general(
        all_normed, grad_pre, (((0,), (0,)), ((), ())), preferred_element_type=jnp.float32
    )
    return (up_product, down_product)


def solution(mesh):
    return jax.shard_map(
        on_device,
        mesh=mesh,
        in_specs=(
            P("dp", "tensor"),
            P("tensor"),
            P("tensor"),
            P("tensor", "dp"),
            P("dp"),
            P("dp", "tensor"),
            P("tensor"),
            P("dp", "tensor"),
            P("tensor", "dp"),
            P("dp", "tensor"),
        ),
        out_specs=(P("tensor", "dp"), P("dp", "tensor")),
        check_vma=False,
    )
```

profile of v0, /device:TPU:1, one launch (start us, length us, event | category | flops | bytes accessed | tf_op | source)
XLA Modules:
  0.0 637.0 jit_solution(9508748308312653953)
XLA Ops:
  7.2 0.0 copy-start
  7.2 0.0 all-gather.4.cloned.1.call-start
  7.2 1.0 convert_reduce_fusion
  8.2 15.0 %all-reduce.3 = (f32[32]{0:T(128)S(1)}, f32[32]{0:T(128)S(1)}) all-reduce(f32[32]{0:T(128)S(1)} %get-tuple-element.9, f32[32]{0:T(128)S(1)} %get-tuple-element.8), channel_id=1, replica_groups=mesh['dp'=32,'tensor'=8] {'tensor'}, use_global_device_ids=true, to_apply=%region_3.0 | all-reduce | flops 64 | bytes 512 | tf_op jit(solution)/shard_map/psum | solution.py:41
  23.3 1.5 fusion.8
  24.8 0.0 all-gather.4.cloned.1.call-update
  24.8 0.0 all-reduce.7.cloned.1.call-start
  24.9 74.0 %all-gather.4.cloned.1.call-done = bf16[1024,768]{1,0:T(8,128)(2,1)} async-done(((bf16[32,768]{1,0:T(8,128)(2,1)}), bf16[1024,768]{1,0:T(8,128)(2,1)}) %all-gather.4.cloned.1.call-update) | async-done | bytes 1572880 | tf_op jit(solution)/shard_map/all_gather | solution.py:46
  98.8 0.0 copy-start.8
  98.8 4.9 fusion.14
  103.7 0.0 copy-done.8
  103.7 4.4 fusion.12
  108.1 0.0 copy-start.7
  108.1 0.0 all-reduce.7.cloned.1.call-update
  108.1 0.0 reduce-scatter.7.cloned.1.call-start
  108.1 91.1 %all-reduce.7.cloned.1.call-done = (f32[1024,768]{1,0:T(8,128)}, f32[1024,768]{1,0:T(8,128)}) async-done(((f32[1024,768]{1,0:T(8,128)}, f32[1024,768]{1,0:T(8,128)}), (f32[1024,768]{1,0:T(8,128)}, f32[1024,768]{1,0:T(8,128)})) %all-reduce.7.cloned.1.call-update) | async-done | bytes 6291472 | tf_op jit(solution)/shard_map/psum | solution.py:50
  199.2 0.0 copy-done.7
  199.2 3.0 multiply_convert_fusion.1
  202.2 0.0 copy-start.1
  202.2 0.0 copy-done
  202.2 0.0 copy-start.2
  202.2 1.4 fusion.13
  203.7 0.2 copy-done.1
  203.9 1.4 copy-done.2
  205.2 0.0 copy-start.3
  205.2 1.4 fusion.4
  206.7 0.0 copy-done.3
  206.7 1.4 convolution_add_fusion
  208.1 3.2 pad_maximum_fusion
  211.4 6.6 %copy.16 = f32[1024,1536]{1,0:T(8,128)} copy(f32[1024,1536]{0,1:T(8,128)} %pad_maximum_fusion) | data formatting | bytes 12582912
  218.0 0.0 copy-start.6
  218.0 0.0 copy-start.4
  218.0 0.0 copy-start.5
  218.0 0.0 reduce-scatter.7.cloned.1.call-update
  218.0 0.0 all-gather.6.cloned.1.call-start
  218.1 0.6 copy-done.6
  218.7 218.9 %reduce-scatter.7.cloned.1.call-done = f32[32,1536]{1,0:T(8,128)} async-done(((f32[1024,1536]{1,0:T(8,128)}), f32[32,1536]{1,0:T(8,128)}) %reduce-scatter.7.cloned.1.call-update) | async-done | bytes 196624 | tf_op jit(solution)/shard_map/reduce_scatter | solution.py:63
  437.6 0.0 copy-done.4
  437.6 1.0 fusion.11
  438.6 16.9 %all-reduce.2 = (f32[32]{0:T(128)S(1)}, f32[32]{0:T(128)S(1)}) all-reduce(f32[32]{0:T(128)S(1)} %get-tuple-element.7, f32[32]{0:T(128)S(1)} %get-tuple-element.6), channel_id=1, replica_groups=mesh['dp'=32,'tensor'=8] {'tensor'}, use_global_device_ids=true, to_apply=%region_12.0 | all-reduce | flops 64 | bytes 512 | tf_op jit(solution)/shard_map/psum | solution.py:70
  455.5 1.1 slice_reduce_fusion
  456.6 12.4 %all-reduce.1 = (f32[32]{0:T(128)S(1)}, f32[32]{0:T(128)S(1)}) all-reduce(f32[32]{0:T(128)S(1)} %get-tuple-element.3, f32[32]{0:T(128)S(1)} %get-tuple-element.2), channel_id=1, replica_groups=mesh['dp'=32,'tensor'=8] {'tensor'}, use_global_device_ids=true, to_apply=%region_14.0 | all-reduce | flops 64 | bytes 512 | tf_op jit(solution)/shard_map/psum | solution.py:74
  469.0 0.0 copy-done.5
  469.0 1.1 fusion.10
  470.1 12.4 %all-reduce = (f32[32]{0:T(128)S(1)}, f32[32]{0:T(128)S(1)}) all-reduce(f32[32]{0:T(128)S(1)} %get-tuple-element.5, f32[32]{0:T(128)S(1)} %get-tuple-element.4), channel_id=1, replica_groups=mesh['dp'=32,'tensor'=8] {'tensor'}, use_global_device_ids=true, to_apply=%region_18.0 | all-reduce | flops 64 | bytes 512 | tf_op jit(solution)/shard_map/psum | solution.py:83
  482.6 0.7 multiply_convert_fusion.4
  483.3 0.0 all-gather.6.cloned.1.call-update
  483.3 0.0 reduce-scatter.5.cloned.1.call-start
  483.3 68.7 %all-gather.6.cloned.1.call-done = bf16[1024,768]{1,0:T(8,128)(2,1)} async-done(((bf16[32,768]{1,0:T(8,128)(2,1)}), bf16[1024,768]{1,0:T(8,128)(2,1)}) %all-gather.6.cloned.1.call-update) | async-done | bytes 1572880 | tf_op jit(solution)/shard_map/all_gather | solution.py:94
  552.1 4.5 fusion.15
  556.6 0.0 reduce-scatter.5.cloned.1.call-update
  556.6 0.2 all-gather.8.cloned.1.call-start
  556.8 1.0 dynamic-slice_convert_fusion
  557.9 36.3 %reduce-scatter.5.cloned.1.call-done = f32[128,768]{1,0:T(8,128)} async-done(((f32[1024,768]{1,0:T(8,128)}), f32[128,768]{1,0:T(8,128)}) %reduce-scatter.5.cloned.1.call-update) | async-done | bytes 393232 | tf_op jit(solution)/shard_map/reduce_scatter | solution.py:101
  594.1 1.7 multiply_convert_fusion.3
  595.8 0.0 all-gather.8.cloned.1.call-update
  595.9 4.3 fusion.17
  600.1 25.4 %all-gather.8.cloned.1.call-done = bf16[1024,768]{1,0:T(8,128)(2,1)} async-done(((bf16[128,768]{1,0:T(8,128)(2,1)}), bf16[1024,768]{1,0:T(8,128)(2,1)}) %all-gather.8.cloned.1.call-update) | async-done | bytes 1572880 | tf_op jit(solution)/shard_map/all_gather | solution.py:103
  625.5 4.7 fusion.16
  (6 shorter events, 0.0 us)
Async XLA Ops:
  7.2 195.0 %copy-start = (bf16[768,768]{1,0:T(8,128)(2,1)S(1)}, bf16[768,768]{1,0:T(8,128)(2,1)}, u32[]{:S(2)}) copy-start(bf16[768,768]{1,0:T(8,128)(2,1)} %param.15) | copy-start | bytes 3538948
  7.2 91.7 %all-gather.4.cloned.1.call-start = ((), (), s32[]{:S(2)}) async-start(), calls=%async_computation.2 | async-start | bytes 1622016 | tf_op jit(solution)/shard_map/all_gather | solution.py:46
  24.8 174.4 %all-reduce.7.cloned.1.call-start = ((), (), s32[]{:S(2)}) async-start(), calls=%async_computation.7 | async-start | bytes 12582912 | tf_op jit(solution)/shard_map/psum | solution.py:50
  98.8 4.9 copy-start.8
  108.1 91.1 %copy-start.7 = (f32[768]{0:T(1024)S(1)}, f32[768]{0:T(1024)}, u32[]{:S(2)}) copy-start(f32[768]{0:T(1024)} %param.14) | copy-start | bytes 9220
  108.1 329.5 %reduce-scatter.7.cloned.1.call-start = ((), (), s32[]{:S(2)}) async-start(), calls=%async_computation.6 | async-start | bytes 6488064 | tf_op jit(solution)/shard_map/reduce_scatter | solution.py:63
  202.2 1.7 copy-start.1
  202.2 3.0 copy-start.2
  205.2 1.4 copy-start.3
  218.0 0.7 copy-start.6
  218.0 219.6 %copy-start.4 = (bf16[32,768]{1,0:T(8,128)(2,1)S(1)}, bf16[32,768]{1,0:T(8,128)(2,1)}, u32[]{:S(2)}) copy-start(bf16[32,768]{1,0:T(8,128)(2,1)} %param.10) | copy-start | bytes 147460
  218.0 251.0 %copy-start.5 = (f32[32,768]{1,0:T(8,128)S(1)}, f32[32,768]{1,0:T(8,128)}, u32[]{:S(2)}) copy-start(f32[32,768]{1,0:T(8,128)} %param.17) | copy-start | bytes 294916
  218.0 334.1 %all-gather.6.cloned.1.call-start = ((), (), s32[]{:S(2)}) async-start(), calls=%async_computation.3 | async-start | bytes 1622016 | tf_op jit(solution)/shard_map/all_gather | solution.py:94
  483.3 110.8 %reduce-scatter.5.cloned.1.call-start = ((), (), s32[]{:S(2)}) async-start(), calls=%async_computation.4 | async-start | bytes 3538944 | tf_op jit(solution)/shard_map/reduce_scatter | solution.py:101
  556.6 68.9 %all-gather.8.cloned.1.call-start = ((), (), s32[]{:S(2)}) async-start(), calls=%async_computation.5 | async-start | bytes 1769472 | tf_op jit(solution)/shard_map/all_gather | solution.py:103
Sparse Core Ops, SparseCore 0:
  24.9 73.8 all-gather.3
  108.2 90.9 all-reduce.6
  218.1 219.3 reduce-scatter.6
  483.4 68.6 all-gather.5
  556.7 37.3 reduce-scatter.4
  596.5 28.8 all-gather.7
where the time goes:
time: 638 us; the launch traced here: 637 us
  waiting for transfers between devices  514 us (81%)
  blocking collectives  56.8 us (9%)
  matrix products  27 us (4%)
  other arithmetic  14.4 us (2%)
  between operations  14.2 us (2%)
  local copies, waits for them, and re-layouts  9.84 us (2%)
    reduce_scatter x1, waiting for transfers between devices, on_device(): lax.psum_scatter(jnp.concatenate([primal, tangent], axis=1), 'dp', scatte...  219 us
    psum x1, waiting for transfers between devices, on_device(): pre_total, tangent_total = lax.psum((pre_part, tangent_part), 'tensor')  91.1 us
    all_gather x1, waiting for transfers between devices, on_device(): all_normed = lax.all_gather(normed, 'dp', axis=0, tiled=True)  74 us
    all_gather x1, waiting for transfers between devices, on_device(): all_cotangent = lax.all_gather(cotangent, 'dp', axis=0, tiled=True)  68.7 us
    reduce_scatter x1, waiting for transfers between devices, on_device(): lax.psum_scatter(back_part, 'tensor', scatter_dimension=0, tiled=True)  36.3 us
    all_gather x1, waiting for transfers between devices, on_device(): grad_pre = lax.all_gather(grad_share, 'tensor', axis=0, tiled=True)  25.4 us
    psum x1, blocking collectives, on_device(): lax.psum((row_total(output), row_total(output * output)), 'tensor')  16.9 us
    psum x1, blocking collectives, on_device(): lax.psum((row_total(source), row_total(source * source)), 'tensor')  15 us
  transfers between devices with their start and end apart: 6, of which 6 were waited for; matrix products, arithmetic and copies ran while one was open for 1% of the time, Pallas kernels for 0%

commit v1 on v0

--- a/solution.py
+++ b/solution.py
@@ -43,7 +43,9 @@
     spread_in = square_in / model_width - center_in * center_in
     inverse_in = lax.rsqrt(spread_in + epsilon)[:, None]
     normed = ((source - center_in[:, None]) * inverse_in * gain_in + shift_in).astype(jnp.bfloat16)
-    all_normed = lax.all_gather(normed, "dp", axis=0, tiled=True)
+    all_normed = jnp.concatenate(
+        lax.all_to_all(jnp.stack([normed] * lax.axis_size("dp")), "dp", 0, 0), axis=0
+    )
     pre_part = jnp.dot(all_normed, up_weight, preferred_element_type=jnp.float32)
     tangent_part = jnp.dot(all_normed, up_tangent, preferred_element_type=jnp.float32)
     share_rows = all_normed.shape[0] // lax.axis_size("tensor")

time: 638 us -> 603 us (0.945)
  waiting for transfers between devices: 514 us -> 441 us
  blocking collectives: 56.8 us -> 100 us
    all_gather x1 -> x0, waiting for transfers between devices: 74 us -> none  [on_device(): all_normed = lax.all_gather(normed, 'dp', axis=0, tiled=True)]
    all_to_all x0 -> x1, blocking collectives: none -> 43.9 us  [on_device(): lax.all_to_all(jnp.stack([normed] * lax.axis_size('dp')), 'dp', 0, 0)]
  transfers between devices with their start and end apart: 6 -> 5, of which waited for: 6 -> 5; matrix products, arithmetic and copies ran while one was open for 1% -> 1% of each run, Pallas kernels for 0% -> 0%
where the time goes in v1:
time: 603 us
  waiting for transfers between devices  441 us (73%)
  blocking collectives  100 us (17%)
  matrix products  23.9 us (4%)
  between operations  13.9 us (2%)
  other arithmetic  13.8 us (2%)
  local copies, waits for them, and re-layouts  10 us (2%)
    reduce_scatter x1, waiting for transfers between devices, on_device(): lax.psum_scatter(jnp.concatenate([primal, tangent], axis=1), 'dp', scatte...  219 us
    psum x1, waiting for transfers between devices, on_device(): pre_total, tangent_total = lax.psum((pre_part, tangent_part), 'tensor')  90.8 us
    all_gather x1, waiting for transfers between devices, on_device(): all_cotangent = lax.all_gather(cotangent, 'dp', axis=0, tiled=True)  68.7 us
    all_to_all x1, blocking collectives, on_device(): lax.all_to_all(jnp.stack([normed] * lax.axis_size('dp')), 'dp', 0, 0)  43.9 us
    reduce_scatter x1, waiting for transfers between devices, on_device(): lax.psum_scatter(back_part, 'tensor', scatter_dimension=0, tiled=True)  36.3 us
    all_gather x1, waiting for transfers between devices, on_device(): grad_pre = lax.all_gather(grad_share, 'tensor', axis=0, tiled=True)  25.4 us
    psum x1, blocking collectives, on_device(): lax.psum((row_total(output), row_total(output * output)), 'tensor')  16.4 us
    psum x1, blocking collectives, on_device(): lax.psum((row_total(source), row_total(source * source)), 'tensor')  15 us
  transfers between devices with their start and end apart: 5, of which 5 were waited for; matrix products, arithmetic and copies ran while one was open for 1% of the time, Pallas kernels for 0%

profile of v1, /device:TPU:1, one launch (start us, length us, event | category | flops | bytes accessed | tf_op | source)
XLA Modules:
  0.0 602.7 jit_solution(5891099124813608627)
XLA Ops:
  7.2 0.0 copy-start
  7.2 0.0 all-reduce.7.cloned.1.call-start
  7.2 1.0 convert_reduce_fusion
  8.2 15.0 %all-reduce.3 = (f32[32]{0:T(128)S(1)}, f32[32]{0:T(128)S(1)}) all-reduce(f32[32]{0:T(128)S(1)} %get-tuple-element.9, f32[32]{0:T(128)S(1)} %get-tuple-element.8), channel_id=1, replica_groups=mesh['dp'=32,'tensor'=8] {'tensor'}, use_global_device_ids=true, to_apply=%region_3.0 | all-reduce | flops 64 | bytes 512 | tf_op jit(solution)/shard_map/psum | solution.py:41
  23.3 0.9 fusion.8
  24.2 0.2 stack.2
  24.3 0.0 copy-start.9
  24.4 43.9 %all_to_all.5 = bf16[32,32,768]{2,1,0:T(8,128)(2,1)S(1)} all-to-all(bf16[32,32,768]{2,1,0:T(8,128)(2,1)S(1)} %stack.2), channel_id=1, replica_groups=mesh['dp'=32,'tensor'=8] {'dp'}, dimensions={0} | all-to-all | bytes 3145728 | tf_op jit(solution)/shard_map/all_to_all | solution.py:47
  68.3 0.0 copy-start.3
  68.3 0.0 copy-done.9
  68.3 0.0 copy-start.10
  68.3 3.0 fusion.14
  71.3 0.0 copy-done.3
  71.3 0.0 copy-done.10
  71.3 3.1 fusion.12
  74.4 0.0 copy-start.8
  74.4 0.0 all-reduce.7.cloned.1.call-update
  74.4 0.0 reduce-scatter.7.cloned.1.call-start
  74.5 90.8 %all-reduce.7.cloned.1.call-done = (f32[1024,768]{1,0:T(8,128)}, f32[1024,768]{1,0:T(8,128)}) async-done(((f32[1024,768]{1,0:T(8,128)}, f32[1024,768]{1,0:T(8,128)}), (f32[1024,768]{1,0:T(8,128)}, f32[1024,768]{1,0:T(8,128)})) %all-reduce.7.cloned.1.call-update) | async-done | bytes 6291472 | tf_op jit(solution)/shard_map/psum | solution.py:52
  165.3 0.0 copy-done.8
  165.3 3.0 multiply_convert_fusion.1
  168.2 0.0 copy-start.1
  168.2 0.0 copy-done
  168.3 0.0 copy-start.2
  168.3 1.4 fusion.13
  169.7 0.2 copy-done.1
  169.9 1.4 copy-done.2
  171.3 0.0 copy-start.4
  171.3 1.4 fusion.4
  172.7 0.0 copy-done.4
  172.7 1.4 convolution_add_fusion
  174.2 3.2 pad_maximum_fusion
  177.4 6.6 %copy.21 = f32[1024,1536]{1,0:T(8,128)} copy(f32[1024,1536]{0,1:T(8,128)} %pad_maximum_fusion) | data formatting | bytes 12582912
  184.0 0.0 copy-start.7
  184.0 0.0 copy-start.5
  184.0 0.0 copy-start.6
  184.0 0.0 reduce-scatter.7.cloned.1.call-update
  184.0 0.0 all-gather.3.cloned.1.call-start
  184.1 0.6 copy-done.7
  184.7 219.3 %reduce-scatter.7.cloned.1.call-done = f32[32,1536]{1,0:T(8,128)} async-done(((f32[1024,1536]{1,0:T(8,128)}), f32[32,1536]{1,0:T(8,128)}) %reduce-scatter.7.cloned.1.call-update) | async-done | bytes 196624 | tf_op jit(solution)/shard_map/reduce_scatter | solution.py:65
  404.1 0.0 copy-done.5
  404.1 1.0 fusion.11
  405.1 16.4 %all-reduce.2 = (f32[32]{0:T(128)S(1)}, f32[32]{0:T(128)S(1)}) all-reduce(f32[32]{0:T(128)S(1)} %get-tuple-element.7, f32[32]{0:T(128)S(1)} %get-tuple-element.6), channel_id=1, replica_groups=mesh['dp'=32,'tensor'=8] {'tensor'}, use_global_device_ids=true, to_apply=%region_12.0 | all-reduce | flops 64 | bytes 512 | tf_op jit(solution)/shard_map/psum | solution.py:72
  421.5 1.1 slice_reduce_fusion
  422.6 12.4 %all-reduce.1 = (f32[32]{0:T(128)S(1)}, f32[32]{0:T(128)S(1)}) all-reduce(f32[32]{0:T(128)S(1)} %get-tuple-element.3, f32[32]{0:T(128)S(1)} %get-tuple-element.2), channel_id=1, replica_groups=mesh['dp'=32,'tensor'=8] {'tensor'}, use_global_device_ids=true, to_apply=%region_14.0 | all-reduce | flops 64 | bytes 512 | tf_op jit(solution)/shard_map/psum | solution.py:76
  435.0 0.0 copy-done.6
  435.0 1.1 fusion.10
  436.1 12.4 %all-reduce = (f32[32]{0:T(128)S(1)}, f32[32]{0:T(128)S(1)}) all-reduce(f32[32]{0:T(128)S(1)} %get-tuple-element.5, f32[32]{0:T(128)S(1)} %get-tuple-element.4), channel_id=1, replica_groups=mesh['dp'=32,'tensor'=8] {'tensor'}, use_global_device_ids=true, to_apply=%region_18.0 | all-reduce | flops 64 | bytes 512 | tf_op jit(solution)/shard_map/psum | solution.py:85
  448.6 0.7 multiply_convert_fusion.4
  449.3 0.0 all-gather.3.cloned.1.call-update
  449.3 0.0 reduce-scatter.5.cloned.1.call-start
  449.4 68.7 %all-gather.3.cloned.1.call-done = bf16[1024,768]{1,0:T(8,128)(2,1)} async-done(((bf16[32,768]{1,0:T(8,128)(2,1)}), bf16[1024,768]{1,0:T(8,128)(2,1)}) %all-gather.3.cloned.1.call-update) | async-done | bytes 1572880 | tf_op jit(solution)/shard_map/all_gather | solution.py:96
  518.1 4.5 fusion.15
  522.6 0.0 reduce-scatter.5.cloned.1.call-update
  522.6 0.2 all-gather.5.cloned.1.call-start
  522.8 1.0 dynamic-slice_convert_fusion
  523.9 36.3 %reduce-scatter.5.cloned.1.call-done = f32[128,768]{1,0:T(8,128)} async-done(((f32[1024,768]{1,0:T(8,128)}), f32[128,768]{1,0:T(8,128)}) %reduce-scatter.5.cloned.1.call-update) | async-done | bytes 393232 | tf_op jit(solution)/shard_map/reduce_scatter | solution.py:103
  560.1 1.7 multiply_convert_fusion.3
  561.8 0.0 all-gather.5.cloned.1.call-update
  561.9 4.3 fusion.17
  566.1 25.4 %all-gather.5.cloned.1.call-done = bf16[1024,768]{1,0:T(8,128)(2,1)} async-done(((bf16[128,768]{1,0:T(8,128)(2,1)}), bf16[1024,768]{1,0:T(8,128)(2,1)}) %all-gather.5.cloned.1.call-update) | async-done | bytes 1572880 | tf_op jit(solution)/shard_map/all_gather | solution.py:105
  591.5 4.7 fusion.16
  (6 shorter events, 0.0 us)
Async XLA Ops:
  7.2 161.1 %copy-start = (bf16[768,768]{1,0:T(8,128)(2,1)S(1)}, bf16[768,768]{1,0:T(8,128)(2,1)}, u32[]{:S(2)}) copy-start(bf16[768,768]{1,0:T(8,128)(2,1)} %param.15) | copy-start | bytes 3538948
  7.2 158.1 %all-reduce.7.cloned.1.call-start = ((), (), s32[]{:S(2)}) async-start(), calls=%async_computation.7 | async-start | bytes 12582912 | tf_op jit(solution)/shard_map/psum | solution.py:52
  24.3 44.0 %copy-start.9 = (bf16[768,768]{1,0:T(8,128)(2,1)S(1)}, bf16[768,768]{1,0:T(8,128)(2,1)}, u32[]{:S(2)}) copy-start(bf16[768,768]{1,0:T(8,128)(2,1)} %param.18) | copy-start | bytes 3538948
  68.3 3.0 copy-start.3
  68.3 3.0 copy-start.10
  74.4 90.8 %copy-start.8 = (f32[768]{0:T(1024)S(1)}, f32[768]{0:T(1024)}, u32[]{:S(2)}) copy-start(f32[768]{0:T(1024)} %param.14) | copy-start | bytes 9220
  74.4 329.6 %reduce-scatter.7.cloned.1.call-start = ((), (), s32[]{:S(2)}) async-start(), calls=%async_computation.6 | async-start | bytes 6488064 | tf_op jit(solution)/shard_map/reduce_scatter | solution.py:65
  168.2 1.7 copy-start.1
  168.3 3.0 copy-start.2
  171.3 1.4 copy-start.4
  184.0 0.7 copy-start.7
  184.0 220.0 %copy-start.5 = (bf16[32,768]{1,0:T(8,128)(2,1)S(1)}, bf16[32,768]{1,0:T(8,128)(2,1)}, u32[]{:S(2)}) copy-start(bf16[32,768]{1,0:T(8,128)(2,1)} %param.10) | copy-start | bytes 147460
  184.0 251.0 %copy-start.6 = (f32[32,768]{1,0:T(8,128)S(1)}, f32[32,768]{1,0:T(8,128)}, u32[]{:S(2)}) copy-start(f32[32,768]{1,0:T(8,128)} %param.17) | copy-start | bytes 294916
  184.0 334.0 %all-gather.3.cloned.1.call-start = ((), (), s32[]{:S(2)}) async-start(), calls=%async_computation.3 | async-start | bytes 1622016 | tf_op jit(solution)/shard_map/all_gather | solution.py:96
  449.3 110.8 %reduce-scatter.5.cloned.1.call-start = ((), (), s32[]{:S(2)}) async-start(), calls=%async_computation.4 | async-start | bytes 3538944 | tf_op jit(solution)/shard_map/reduce_scatter | solution.py:103
  522.6 68.9 %all-gather.5.cloned.1.call-start = ((), (), s32[]{:S(2)}) async-start(), calls=%async_computation.5 | async-start | bytes 1769472 | tf_op jit(solution)/shard_map/all_gather | solution.py:105
Sparse Core Ops, SparseCore 0:
  74.6 90.6 all-reduce.6
  184.2 219.8 reduce-scatter.6
  449.4 68.6 all-gather.2
  522.7 37.3 reduce-scatter.4
  562.5 28.8 all-gather.4
